TPU v7x, 32 devices: a whole 2x2x4 slice. The times are simulated.
32 devices in a mesh: groups: 2 (over y), date: 8 (over z, x), pix: 2 (over core).
Axes of the slice: x: 2, y: 2, z: 4, core: 2. Of those that a mesh axis runs over, the one named last changes fastest.
Arguments:
- slc_tiles: bfloat16 [32, 2, 64, 1024], P(('groups', 'date'), None, None, 'pix'), parts along dimension 0, may hold values from -8 to 8
- pair_list: int32 [128, 2], P(('groups', 'date')), parts along dimension 0, may hold values from 0 to 15, as said below
- band_cuts: int32 [128, 2], P(('groups', 'date')), parts along dimension 0, may hold values from 0 to 127
- look_sizes: int32 [128, 2], P(('groups', 'date')), parts along dimension 0, may hold values from 1 to 16, as said below
Outputs:
- interferogram: float32 [128, 2, 64, 1024], P(('groups', 'date'), None, None, 'pix'), parts along dimension 0
- coherence: float32 [128, 64, 1024], P(('groups', 'date'), None, 'pix'), parts along dimension 0
There are 2 independent parts, one for each index of `groups`. A program takes and returns all parts, laid end to end along the dimension named above; each array names one. Nothing has to cross between parts.
Inputs may be any that keep to these rules, and one draw needn't show every extreme that they name: `pair_list`: in aligned block r of 8 rows the first column is a date of r * 2 to r * 2 + 1 and the second another date at most 6 away from it; the first row of every block is exactly 6 away. `look_sizes`: column 0 is 1 to 4, column 1 is 1 to 16; the first row of every aligned block of 8 rows holds 4 and 16.
All inputs are finite; a program needn't handle non-finite values.
Results may differ from a plain program's by a relative error of at most 0.004.
Values may be sent and summed in bfloat16 or wider, within the bound.
A program may use at most 64 MiB of HBM per device.

v0:
```python
import math

import jax
import jax.numpy as jnp
from jax import lax
from jax.sharding import PartitionSpec as P

RBLK = 512
HR = 16
REACH = 3


def shifted(x, axis, by):
    count = lax.axis_size(axis)
    pairs = [(i, i + by) for i in range(count) if 0 <= i + by < count]
    return lax.ppermute(x, axis, pairs)


def extended_2(x, sides, width):
    for axis, dim in sides:
        count, length = (lax.axis_size(axis), x.shape[dim])
        up = [(i, (i + 1) % count) for i in range(count - 1)]
        down = [(j, i) for i, j in up]
        last = lax.slice_in_dim(x, length - width, length, axis=dim)
        leading = lax.slice_in_dim(x, 0, width, axis=dim)
        before = lax.ppermute(last, axis, up)
        after = lax.ppermute(leading, axis, down)
        x = jnp.concatenate([before, x, after], axis=dim)
    return x


def dft_tables(length):
    counter = jnp.arange(length, dtype=jnp.int32)
    product = counter[:, None] * counter[None, :] % length
    angles = product.astype(jnp.float32) * (2.0 * math.pi / length)
    return (jnp.cos(angles), jnp.sin(angles))


def transform(tiles, table_high, table_low):
    length = table_high.shape[0] // 2
    count = tiles.shape[0]
    azimuth_rows = tiles.shape[2]
    width = tiles.shape[3]
    values = tiles.reshape(count, 2, azimuth_rows, width // length, length)
    values = values.transpose(0, 2, 3, 1, 4).reshape(
        count, azimuth_rows, width // length, 2 * length
    )
    return jnp.dot(values, table_high, preferred_element_type=jnp.float32) + jnp.dot(
        values, table_low, preferred_element_type=jnp.float32
    )


def products(fields):
    values = fields.astype(jnp.float32)
    first_re = values[:, 0, 0]
    first_im = values[:, 0, 1]
    second_re = values[:, 1, 0]
    second_im = values[:, 1, 1]
    return jnp.stack(
        [
            first_re * second_re + first_im * second_im,
            first_im * second_re - first_re * second_im,
            first_re * first_re + first_im * first_im,
            second_re * second_re + second_im * second_im,
        ],
        1,
    )


def body(slc_tiles, pair_list, band_cuts, look_sizes):
    length = RBLK
    cosine, sine_table = dft_tables(length)
    forward = jnp.concatenate(
        [jnp.concatenate([cosine, -sine_table], 1), jnp.concatenate([sine_table, cosine], 1)], 0
    )
    inverse = (
        jnp.concatenate(
            [jnp.concatenate([cosine, sine_table], 1), jnp.concatenate([-sine_table, cosine], 1)], 0
        )
        / length
    )
    forward_high = forward.astype(jnp.bfloat16)
    forward_low = (forward - forward_high.astype(jnp.float32)).astype(jnp.bfloat16)
    owned = slc_tiles.shape[0]
    azimuth_rows = slc_tiles.shape[2]
    width = slc_tiles.shape[3]
    blocks = width // length
    pair_count = pair_list.shape[0]
    below_list = []
    above_list = []
    for distance in range(1, REACH + 1):
        for direction in (1, -1):
            moved_piece = shifted(slc_tiles, "date", direction * distance)
            if direction == 1:
                below_list.append(moved_piece)
            else:
                above_list.append(moved_piece)
    window = transform(
        jnp.concatenate(below_list[::-1] + [slc_tiles] + above_list, 0), forward_high, forward_low
    )
    device = lax.axis_index("date")
    first_date = (device - REACH) * owned
    picks = (pair_list - first_date).reshape(-1)
    chosen = jnp.take(window, picks, axis=0).reshape(
        pair_count, 2, azimuth_rows, blocks, 2 * length
    )
    freq_index = (jnp.arange(length, dtype=jnp.int32) + length // 2) % length
    keep_mask = (
        (freq_index[None, :] >= band_cuts[:, 0:1])
        & (freq_index[None, :] < length - band_cuts[:, 1:2])
    ).astype(jnp.float32)
    keep_both = jnp.concatenate([keep_mask, keep_mask], 1)[:, None, None, None, :]
    fields = jnp.dot(chosen * keep_both, inverse, precision=lax.Precision.HIGH).astype(jnp.bfloat16)
    fields = fields.reshape(pair_count, 2, azimuth_rows, blocks, 2, length)
    fields = fields.transpose(0, 1, 4, 2, 3, 5).reshape(pair_count, 2, 2, azimuth_rows, width)
    extended = extended_2(fields, (("pix", 4),), HR)
    quantity = products(extended)
    tile_width = math.gcd(width, 128)
    tile_count = width // tile_width
    tile_cols = jnp.arange(tile_width + 2 * HR, dtype=jnp.int32)
    tile_out = jnp.arange(tile_width, dtype=jnp.int32)
    col_gap = jnp.abs(tile_cols[:, None] - HR - tile_out[None, :])
    azimuths = jnp.arange(azimuth_rows, dtype=jnp.int32)
    row_gap = jnp.abs(azimuths[:, None] - azimuths[None, :])

    def multilook(items):
        quantity_pair, halves = items
        range_band = (col_gap <= halves[1]).astype(jnp.float32)
        azimuth_band = (row_gap <= halves[0]).astype(jnp.float32)
        windows = jnp.stack(
            [
                quantity_pair[:, :, start * tile_width : start * tile_width + tile_width + 2 * HR]
                for start in range(tile_count)
            ],
            2,
        )
        partial_sum = jnp.einsum("qatc,cd->qatd", windows, range_band, precision=lax.Precision.HIGH)
        partial_sum = partial_sum.reshape(4, azimuth_rows, width)
        sums = jnp.einsum("ba,qad->qbd", azimuth_band, partial_sum, precision=lax.Precision.HIGH)
        window_count = ((2 * halves[0] + 1) * (2 * halves[1] + 1)).astype(jnp.float32)
        interferogram = sums[0:2] / window_count
        magnitude = jnp.sqrt(sums[0] * sums[0] + sums[1] * sums[1])
        coherence = magnitude / (jnp.sqrt(sums[2] * sums[3]) + 0.25 * window_count)
        return (interferogram, coherence)

    interferogram, coherence = lax.map(multilook, (quantity, look_sizes))
    return (interferogram, coherence)


def solution(mesh):
    placed = (
        P(("groups", "date"), None, None, "pix"),
        P(("groups", "date"), None),
        P(("groups", "date"), None),
        P(("groups", "date"), None),
    )
    return jax.shard_map(
        body,
        mesh=mesh,
        in_specs=placed,
        out_specs=(P(("groups", "date"), None, None, "pix"), P(("groups", "date"), None, "pix")),
        check_vma=False,
    )
```

profile of v0, /device:TPU:7, one launch (start us, length us, event | category | flops | bytes accessed | tf_op | source)
XLA Modules:
  0.0 140.2 jit_solution(14974921348607598588)
XLA Ops:
  0.7 4.3 %collective-permute-start = (bf16[2,2,64,512]{3,2,1,0:T(8,128)(2,1)}, bf16[2,2,64,512]{3,2,1,0:T(8,128)(2,1)S(1)}, u32[]{:S(2)}, u32[]{:S(2)}) collective-permute-start(bf16[2,2,64,512]{3,2,1,0:T(8,128)(2,1)} %param.6), channel_id=1, source_target_pairs={{0,6},{2,8},{4,10},{6,12},{8,14},{1,7},{3,9},{5,11},{7,13},{9,15},... | collective-permute-start | bytes 786440 | tf_op jit(solution)/shard_map/ppermute | solution.py:16
  5.0 3.2 %collective-permute-start.1 = (bf16[2,2,64,512]{3,2,1,0:T(8,128)(2,1)}, bf16[2,2,64,512]{3,2,1,0:T(8,128)(2,1)S(1)}, u32[]{:S(2)}, u32[]{:S(2)}) collective-permute-start(bf16[2,2,64,512]{3,2,1,0:T(8,128)(2,1)} %param.6), channel_id=1, source_target_pairs={{0,4},{2,6},{4,8},{6,10},{8,12},{10,14},{1,5},{3,7},{5,9},{7,11},{... | collective-permute-start | bytes 786440 | tf_op jit(solution)/shard_map/ppermute | solution.py:16
  8.2 3.1 %collective-permute-start.2 = (bf16[2,2,64,512]{3,2,1,0:T(8,128)(2,1)}, bf16[2,2,64,512]{3,2,1,0:T(8,128)(2,1)S(1)}, u32[]{:S(2)}, u32[]{:S(2)}) collective-permute-start(bf16[2,2,64,512]{3,2,1,0:T(8,128)(2,1)} %param.6), channel_id=1, source_target_pairs={{0,2},{2,4},{4,6},{6,8},{8,10},{10,12},{12,14},{1,3},{3,5},{5,7},{... | collective-permute-start | bytes 786440 | tf_op jit(solution)/shard_map/ppermute | solution.py:16
  11.3 2.2 %collective-permute-start.3 = (bf16[2,2,64,512]{3,2,1,0:T(8,128)(2,1)}, bf16[2,2,64,512]{3,2,1,0:T(8,128)(2,1)S(1)}, u32[]{:S(2)}, u32[]{:S(2)}) collective-permute-start(bf16[2,2,64,512]{3,2,1,0:T(8,128)(2,1)} %param.6), channel_id=1, source_target_pairs={{2,0},{4,2},{6,4},{8,6},{10,8},{12,10},{14,12},{3,1},{5,3},{7,5},{... | collective-permute-start | bytes 786440 | tf_op jit(solution)/shard_map/ppermute | solution.py:16
  13.5 1.3 collective-permute-start.4
  14.8 5.3 %fusion.65 = (f32[512,512]{1,0:T(8,128)S(1)}, f32[512,512]{1,0:T(8,128)}) fusion(), kind=kLoop, calls=%fused_computation.81 | loop fusion | flops 3670016 | bytes 2097152 | tf_op jit(solution)/shard_map/sin | solution.py:36
  20.4 4.7 %fusion.67 = f32[512,512]{1,0:T(8,128)} fusion(), kind=kLoop, calls=%fused_computation.83 | loop fusion | flops 3932160 | bytes 1048576 | tf_op jit(solution)/shard_map/neg | solution.py:74
  25.2 1.3 collective-permute-start.5
  26.7 15.4 %collective-permute-done.5 = bf16[2,2,64,512]{3,2,1,0:T(8,128)(2,1)S(1)} collective-permute-done((bf16[2,2,64,512]{3,2,1,0:T(8,128)(2,1)S(1)}, bf16[2,2,64,512]{3,2,1,0:T(8,128)(2,1)S(1)}, u32[]{:S(2)}, u32[]{:S(2)}) %collective-permute-start.5) | collective-permute-done | bytes 262176 | tf_op jit(solution)/shard_map/ppermute | solution.py:16
  42.1 1.9 %copy.21 = bf16[14,64,1,2,512]{4,3,1,0,2:T(2,128)(2,1)S(1)} copy(bf16[14,64,1,2,512]{4,1,3,0,2:T(8,128)(2,1)S(1)} %bitcast.110) | data formatting | bytes 3670016 | tf_op jit(solution)/shard_map/transpose | solution.py:45
  44.0 2.3 %reshape.236 = bf16[14,64,1024]{2,1,0:T(8,128)(2,1)} reshape(bf16[14,64,1,2,512]{4,3,1,0,2:T(2,128)(2,1)S(1)} %copy.21) | data formatting | bytes 3670016 | tf_op jit(solution)/shard_map/reshape.5
  46.4 4.6 %fusion.41 = f32[14,64,1024]{2,1,0:T(8,128)S(1)} fusion(bf16[14,64,1024]{2,1,0:T(8,128)(2,1)} %reshape.236, f32[512,512]{1,0:T(8,128)} %get-tuple-element.87, f32[512,512]{1,0:T(8,128)S(1)} %get-tuple-element.86, f32[512,512]{1,0:T(8,128)} %fusion.67), kind=kOutput, calls=%fused_computation.58 | convolution fusion | flops 1886388224 | bytes 8650752 | tf_op jit(solution)/shard_map/dot_general | solution.py:48
  51.0 3.9 %fusion.54 = f32[14,64,1024]{2,1,0:T(8,128)} fusion(f32[14,64,1024]{2,1,0:T(8,128)S(1)} %fusion.41, bf16[14,64,1024]{2,1,0:T(8,128)(2,1)S(1)} %copy-done, f32[512,512]{1,0:T(8,128)S(1)} %copy-done.1, f32[512,512]{1,0:T(8,128)S(1)} %get-tuple-element.86, f32[512,512]{1,0:T(8,128)S(1)} %copy-done.2), kind=kOutput, calls=%fused_computation.67 | convolution fusion | flops 1888354304 | bytes 12320768 | tf_op jit(solution)/shard_map/dot_general | solution.py:48
  54.9 4.8 %gather_fusion = f32[16,64,1024]{2,1,0:T(8,128)} fusion(f32[14,64,1024]{2,1,0:T(8,128)} %fusion.54, s32[1024]{0:T(1024)S(1)} %pad_clamp_fusion), kind=kCustom, calls=%fused_computation | custom fusion | bytes 8388672 | tf_op jit(solution)/shard_map/jit(_take)/gather | solution.py:104
  59.7 10.3 %fusion.49 = bf16[8,2,64,1024]{3,2,1,0:T(8,128)(2,1)} fusion(f32[512,512]{1,0:T(8,128)S(1)} %copy-done.1, f32[512,512]{1,0:T(8,128)} %fusion.67, f32[512,512]{1,0:T(8,128)S(1)} %get-tuple-element.86, f32[8,2,64,1024]{3,2,1,0:T(8,128)} %bitcast.109, f32[8,1024]{1,0:T(8,128)S(1)} %add_convert_fusion, pred[8,2]{1,0:T(8,128)(4,1)S(1)} %copy.20), kind=kOutput, calls=%fused_computation.66 | convolution fusion | flops 6449790976 | bytes 9469968 | tf_op jit(solution)/shard_map/dot_general | solution.py:113
  70.0 3.3 %reshape.238 = bf16[8,2,64,1,2,512]{5,4,2,1,0,3:T(2,128)(2,1)S(1)} reshape(bf16[8,2,64,1024]{3,2,1,0:T(8,128)(2,1)} %fusion.49) | data formatting | bytes 4194304 | tf_op jit(solution)/shard_map/reshape | solution.py:114
  74.1 1.3 collective-permute-start.6
  75.4 3.9 %collective-permute-start.7 = (bf16[8,2,2,64,16]{4,3,0,2,1:T(8,128)(2,1)S(1)}, bf16[8,2,2,64,16]{4,3,0,2,1:T(8,128)(2,1)S(1)}, u32[]{:S(2)}, u32[]{:S(2)}) collective-permute-start(bf16[8,2,2,64,16]{4,3,0,2,1:T(8,128)(2,1)S(1)} %get-tuple-element.83), channel_id=1, source_target_pairs={{1,0},{3,2},{5,4},{7,6},{9,8},{11,10},{13,12},{15,14},{17,16},{19,... | collective-permute-start | bytes 196616 | tf_op jit(solution)/shard_map/ppermute | solution.py:27
  79.3 1.3 collective-permute-done.7
  80.6 1.3 maximum_convert_fusion
  81.9 0.8 add_bitcast_fusion.2
  82.8 2.7 %pad_maximum_fusion.4 = f32[8,4,64,544]{3,2,1,0:T(8,128)} fusion(f32[8,1,64,544]{3,2,1,0:T(8,128)S(1)} %get-tuple-element.81, f32[8,1,64,544]{3,2,1,0:T(8,128)S(1)} %get-tuple-element.79, f32[8,1,64,544]{3,2,1,0:T(8,128)S(1)} %get-tuple-element.80, f32[8,1,64,544]{3,2,1,0:T(8,128)S(1)} %get-tuple-element.78), kind=kLoop, calls=%fused_computation.44 | loop fusion | flops 3342336 | bytes 8912896 | tf_op jit(solution)/shard_map/stack | solution.py:59
  85.5 54.7 %while.13 = (s32[]{:T(128)}, f32[8,2,64,512]{3,2,1,0:T(8,128)}, f32[8,64,512]{2,1,0:T(8,128)}, f32[8,4,64,544]{3,2,1,0:T(8,128)}, s32[8,2]{0,1:T(2,128)S(1)}, /*...) while((s32[]{:T(128)}, f32[8,2,64,512]{3,2,1,0:T(8,128)}, f32[8,64,512]{2,1,0:T(8,128)}, ...), condition=%wide.region_1.2_spmd.clone, body=%wide.region_0.1_spmd.clone.sunk | while | flops 176988160 | bytes 5834597 | solution.py:146
  85.5 1.1 dynamic-slice_bitcast_fusion.2
  87.4 1.2 convolution_bitcast_fusion.4
  88.6 0.9 convolution_bitcast_fusion.5
  91.6 0.8 fusion.92
  92.3 1.1 dynamic-slice_bitcast_fusion.2
  94.2 1.2 convolution_bitcast_fusion.4
  95.4 0.9 convolution_bitcast_fusion.5
  99.2 1.1 dynamic-slice_bitcast_fusion.2
  101.1 1.2 convolution_bitcast_fusion.4
  102.3 0.9 convolution_bitcast_fusion.5
  106.0 1.1 dynamic-slice_bitcast_fusion.2
  107.9 1.2 convolution_bitcast_fusion.4
  109.1 0.9 convolution_bitcast_fusion.5
  112.8 1.1 dynamic-slice_bitcast_fusion.2
  114.7 1.2 convolution_bitcast_fusion.4
  115.9 0.9 convolution_bitcast_fusion.5
  119.7 1.1 dynamic-slice_bitcast_fusion.2
  121.6 1.2 convolution_bitcast_fusion.4
  122.8 0.9 convolution_bitcast_fusion.5
  126.5 1.1 dynamic-slice_bitcast_fusion.2
  128.4 1.2 convolution_bitcast_fusion.4
  129.6 0.9 convolution_bitcast_fusion.5
  133.3 1.1 dynamic-slice_bitcast_fusion.2
  135.2 1.2 convolution_bitcast_fusion.4
  136.4 0.9 convolution_bitcast_fusion.5
  (81 shorter events, 18.5 us)
Async XLA Ops:
  0.6 24.6 %copy-start.3 = (bf16[2,2,64,512]{3,2,1,0:T(8,128)(2,1)S(1)}, bf16[2,2,64,512]{3,2,1,0:T(8,128)(2,1)}, u32[]{:S(2)}) copy-start(bf16[2,2,64,512]{3,2,1,0:T(8,128)(2,1)} %param.6) | copy-start | bytes 786436
  0.6 19.5 %copy-start.5 = (s32[8,2]{0,1:T(2,128)S(1)}, s32[8,2]{0,1:T(2,128)}, u32[]{:S(2)}) copy-start(s32[8,2]{0,1:T(2,128)} %param.7) | copy-start | bytes 196
  0.6 19.7 %copy-start.6 = (s32[8,2]{0,1:T(2,128)S(1)}, s32[8,2]{0,1:T(2,128)}, u32[]{:S(2)}) copy-start(s32[8,2]{0,1:T(2,128)} %param.8) | copy-start | bytes 196
  0.7 24.5 %collective-permute-start = (bf16[2,2,64,512]{3,2,1,0:T(8,128)(2,1)}, bf16[2,2,64,512]{3,2,1,0:T(8,128)(2,1)S(1)}, u32[]{:S(2)}, u32[]{:S(2)}) collective-permute-start(bf16[2,2,64,512]{3,2,1,0:T(8,128)(2,1)} %param.6), channel_id=1, source_target_pairs={{0,6},{2,8},{4,10},{6,12},{8,14},{1,7},{3,9},{5,11},{7,13},{9,15},... | collective-permute-start | bytes 786440 | tf_op jit(solution)/shard_map/ppermute | solution.py:16
  5.0 21.5 %collective-permute-start.1 = (bf16[2,2,64,512]{3,2,1,0:T(8,128)(2,1)}, bf16[2,2,64,512]{3,2,1,0:T(8,128)(2,1)S(1)}, u32[]{:S(2)}, u32[]{:S(2)}) collective-permute-start(bf16[2,2,64,512]{3,2,1,0:T(8,128)(2,1)} %param.6), channel_id=1, source_target_pairs={{0,4},{2,6},{4,8},{6,10},{8,12},{10,14},{1,5},{3,7},{5,9},{7,11},{... | collective-permute-start | bytes 786440 | tf_op jit(solution)/shard_map/ppermute | solution.py:16
  8.2 18.3 %collective-permute-start.2 = (bf16[2,2,64,512]{3,2,1,0:T(8,128)(2,1)}, bf16[2,2,64,512]{3,2,1,0:T(8,128)(2,1)S(1)}, u32[]{:S(2)}, u32[]{:S(2)}) collective-permute-start(bf16[2,2,64,512]{3,2,1,0:T(8,128)(2,1)} %param.6), channel_id=1, source_target_pairs={{0,2},{2,4},{4,6},{6,8},{8,10},{10,12},{12,14},{1,3},{3,5},{5,7},{... | collective-permute-start | bytes 786440 | tf_op jit(solution)/shard_map/ppermute | solution.py:16
  11.3 15.3 %collective-permute-start.3 = (bf16[2,2,64,512]{3,2,1,0:T(8,128)(2,1)}, bf16[2,2,64,512]{3,2,1,0:T(8,128)(2,1)S(1)}, u32[]{:S(2)}, u32[]{:S(2)}) collective-permute-start(bf16[2,2,64,512]{3,2,1,0:T(8,128)(2,1)} %param.6), channel_id=1, source_target_pairs={{2,0},{4,2},{6,4},{8,6},{10,8},{12,10},{14,12},{3,1},{5,3},{7,5},{... | collective-permute-start | bytes 786440 | tf_op jit(solution)/shard_map/ppermute | solution.py:16
  13.5 13.1 %collective-permute-start.4 = (bf16[2,2,64,512]{3,2,1,0:T(8,128)(2,1)}, bf16[2,2,64,512]{3,2,1,0:T(8,128)(2,1)S(1)}, u32[]{:S(2)}, u32[]{:S(2)}) collective-permute-start(bf16[2,2,64,512]{3,2,1,0:T(8,128)(2,1)} %param.6), channel_id=1, source_target_pairs={{4,0},{6,2},{8,4},{10,6},{12,8},{14,10},{5,1},{7,3},{9,5},{11,7},{... | collective-permute-start | bytes 786440 | tf_op jit(solution)/shard_map/ppermute | solution.py:16
  25.2 16.9 %collective-permute-start.5 = (bf16[2,2,64,512]{3,2,1,0:T(8,128)(2,1)S(1)}, bf16[2,2,64,512]{3,2,1,0:T(8,128)(2,1)S(1)}, u32[]{:S(2)}, u32[]{:S(2)}) collective-permute-start(bf16[2,2,64,512]{3,2,1,0:T(8,128)(2,1)S(1)} %copy-done.3), channel_id=1, source_target_pairs={{6,0},{8,2},{10,4},{12,6},{14,8},{7,1},{9,3},{11,5},{13,7},{15,9},... | collective-permute-start | bytes 786440 | tf_op jit(solution)/shard_map/ppermute | solution.py:16
  46.3 4.6 %copy-start = (bf16[14,64,1024]{2,1,0:T(8,128)(2,1)S(1)}, bf16[14,64,1024]{2,1,0:T(8,128)(2,1)}, u32[]{:S(2)}) copy-start(bf16[14,64,1024]{2,1,0:T(8,128)(2,1)} %reshape.236) | copy-start | bytes 5505028
  46.3 4.6 %copy-start.1 = (f32[512,512]{1,0:T(8,128)S(1)}, f32[512,512]{1,0:T(8,128)}, u32[]{:S(2)}) copy-start(f32[512,512]{1,0:T(8,128)} %get-tuple-element.87) | copy-start | bytes 3145732
  46.3 4.6 %copy-start.2 = (f32[512,512]{1,0:T(8,128)S(1)}, f32[512,512]{1,0:T(8,128)}, u32[]{:S(2)}) copy-start(f32[512,512]{1,0:T(8,128)} %fusion.67) | copy-start | bytes 3145732
  74.1 5.2 %collective-permute-start.6 = (bf16[8,2,2,64,16]{4,3,0,2,1:T(8,128)(2,1)S(1)}, bf16[8,2,2,64,16]{4,3,0,2,1:T(8,128)(2,1)S(1)}, u32[]{:S(2)}, u32[]{:S(2)}) collective-permute-start(bf16[8,2,2,64,16]{4,3,0,2,1:T(8,128)(2,1)S(1)} %get-tuple-element.82), channel_id=1, source_target_pairs={{0,1},{2,3},{4,5},{6,7},{8,9},{10,11},{12,13},{14,15},{16,17},{18,... | collective-permute-start | bytes 196616 | tf_op jit(solution)/shard_map/ppermute | solution.py:26
  75.4 5.2 %collective-permute-start.7 = (bf16[8,2,2,64,16]{4,3,0,2,1:T(8,128)(2,1)S(1)}, bf16[8,2,2,64,16]{4,3,0,2,1:T(8,128)(2,1)S(1)}, u32[]{:S(2)}, u32[]{:S(2)}) collective-permute-start(bf16[8,2,2,64,16]{4,3,0,2,1:T(8,128)(2,1)S(1)} %get-tuple-element.83), channel_id=1, source_target_pairs={{1,0},{3,2},{5,4},{7,6},{9,8},{11,10},{13,12},{15,14},{17,16},{19,... | collective-permute-start | bytes 196616 | tf_op jit(solution)/shard_map/ppermute | solution.py:27
  82.8 2.7 %copy-start.4 = (s32[8,2]{0,1:T(2,128)S(1)}, s32[8,2]{0,1:T(2,128)}, u32[]{:S(2)}) copy-start(s32[8,2]{0,1:T(2,128)} %param.9) | copy-start | bytes 196
where the time goes:
time: 141 us; the launch traced here: 140 us
  matrix products  35.8 us (25%)
  local copies, waits for them, and re-layouts  28.5 us (20%)
  other arithmetic  26.9 us (19%)
  starting transfers between devices  20.6 us (15%)
  waiting for transfers between devices  16.7 us (12%)
  loops' own time  10.7 us (8%)
    ppermute x6, waiting for transfers between devices, shifted(): return lax.ppermute(x, axis, pairs)  15.4 us
    ppermute x6, starting transfers between devices, shifted(): return lax.ppermute(x, axis, pairs)  15.4 us
    dynamic_update_slice x16, other arithmetic, body(): interferogram, coherence = lax.map(multilook, (quantity, look_sizes))  12 us
    another operation x1, loops' own time, body(): interferogram, coherence = lax.map(multilook, (quantity, look_sizes))  10.7 us
    dot_general x1, matrix products, body(): jnp.dot(chosen * keep_both, inverse, precision=lax.Precision.HIGH)  10.3 us
    dot_general x8, matrix products, multilook(): jnp.einsum('qatc,cd->qatd', windows, range_band, precision=lax.Precision....  9.58 us
    squeeze x8, local copies, waits for them, and re-layouts, body(): interferogram, coherence = lax.map(multilook, (quantity, look_sizes))  9.04 us
    dot_general x8, matrix products, multilook(): jnp.einsum('ba,qad->qbd', azimuth_band, partial_sum, precision=lax.Precis...  7.35 us
  transfers between devices with their start and end apart: 8, of which 2 were waited for; matrix products, arithmetic and copies ran while one was open for 7% of the time, Pallas kernels for 0%

commit v1 on v0

v1 whole, which is shorter than its diff:
```python
import functools

import jax
import jax.numpy as jnp
import numpy as np
from jax import lax
from jax.experimental import pallas as pl
from jax.experimental.pallas import tpu as pltpu
from jax.sharding import PartitionSpec as P

MESH = pl.DeviceIdType.MESH
RBLK = 512
SUB = 128
RADIX = RBLK // SUB
REACH = 3
SLOT_REL = (1, -2, 2, 3, -1, -3)


def split(x):
    high = x.astype(jnp.bfloat16)
    return high, (x - high.astype(jnp.float32)).astype(jnp.bfloat16)


def dft_tables():
    count = np.arange(SUB)
    turn = np.exp(-2j * np.pi * (np.outer(count, count) % SUB) / SUB)

    def real_form(m):
        return np.block([[m.real, m.imag], [-m.imag, m.real]]).astype(np.float32)

    def halves(m):
        high = m.astype(jnp.bfloat16)
        return np.stack([high, (m - high.astype(np.float32)).astype(jnp.bfloat16)])

    twiddle = np.exp(-2j * np.pi * np.outer(np.arange(RADIX), count) / RBLK)
    return (
        halves(real_form(turn)),
        halves(real_form(turn.conj() / RBLK)),
        np.stack([twiddle.real, twiddle.imag]).astype(np.float32),
    )


def dot(a, b):
    return jnp.dot(a, b, preferred_element_type=jnp.float32)


def dot3(high, low, table):
    return dot(high, table[0]) + dot(low, table[0]) + dot(high, table[1])


def forward(image, table, twiddle, high_ref, low_ref, index):
    rows = image.shape[1]
    re = [image[0, :, n * SUB : (n + 1) * SUB].astype(jnp.float32) for n in range(RADIX)]
    im = [image[1, :, n * SUB : (n + 1) * SUB].astype(jnp.float32) for n in range(RADIX)]
    sr, si = (re[0] + re[2], im[0] + im[2])
    dr, di = (re[0] - re[2], im[0] - im[2])
    tr, ti = (re[1] + re[3], im[1] + im[3])
    er, ei = (re[1] - re[3], im[1] - im[3])
    parts = [(sr + tr, si + ti), (dr + ei, di - er), (sr - tr, si - ti), (dr - ei, di + er)]
    turned = []
    for k, (pr, pi) in enumerate(parts):
        c, s = (twiddle[0, k : k + 1, :], twiddle[1, k : k + 1, :])
        turned.append(
            jnp.concatenate([pr, pi] if k == 0 else [pr * c - pi * s, pr * s + pi * c], 1)
        )
    high, low = split(jnp.concatenate(turned, 0))
    high, low = split(dot3(high, low, table))
    high_ref[index] = high
    low_ref[index] = low


def inverse(high, low, mask, table, twiddle, rows):
    y = dot3(high * mask, low * mask, table)
    terms = []
    for k in range(RADIX):
        pr = y[k * rows : (k + 1) * rows, :SUB]
        pi = y[k * rows : (k + 1) * rows, SUB:]
        if k:
            c, s = (twiddle[0, k : k + 1, :], twiddle[1, k : k + 1, :])
            pr, pi = (pr * c + pi * s, pi * c - pr * s)
        terms.append((pr, pi))
    (ar, ai), (br, bi), (cr, ci), (er, ei) = terms
    sr, si, dr, di = (ar + cr, ai + ci, ar - cr, ai - ci)
    tr, ti, fr, fi = (br + er, bi + ei, br - er, bi - ei)
    return [(sr + tr, si + ti), (dr - fi, di + fr), (sr - tr, si - ti), (dr + fi, di - fr)]


def field_kernel(
    dates_dev,
    pairs_ref,
    cuts_ref,
    slc_ref,
    fwd_ref,
    inv_ref,
    twiddle_ref,
    fields_ref,
    halo_ref,
    window,
    spec_high,
    spec_low,
    send_sem,
    recv_sem,
    edge_send,
    edge_recv,
):
    owned, _, rows, width = slc_ref.shape
    pair_count = pairs_ref.shape[0]
    group = lax.axis_index("groups")
    me = lax.axis_index("date")
    pix = lax.axis_index("pix")
    sign = 1 - 2 * lax.rem(me, 2)
    partner = me + sign
    ahead = me + 2 * sign
    behind = me - 2 * sign
    has_ahead = (ahead >= 0) & (ahead < dates_dev)
    has_behind = (behind >= 0) & (behind < dates_dev)
    far = me - sign
    has_far = (far >= 0) & (far < dates_dev)
    last = me - 3 * sign
    has_last = (last >= 0) & (last < dates_dev)

    barrier = pltpu.get_barrier_semaphore()

    def greet(date, pixel):
        pl.semaphore_signal(
            barrier, inc=1, device_id=(group, date, pixel), device_id_type=MESH
        )

    greet(partner, pix)
    greet(me, 1 - pix)
    pl.when(has_ahead)(lambda: greet(ahead, pix))
    pl.when(has_behind)(lambda: greet(behind, pix))
    pl.semaphore_wait(barrier, 2 + has_ahead.astype(jnp.int32) + has_behind.astype(jnp.int32))

    def copy(slot, source, d, target):
        src = slc_ref.at[d] if source is None else window.at[source, d]
        return pltpu.make_async_remote_copy(
            src_ref=src,
            dst_ref=window.at[slot, d],
            send_sem=send_sem.at[slot, d],
            recv_sem=recv_sem.at[slot, d],
            device_id=(group, target, pix),
            device_id_type=MESH,
        )

    plan = (
        (None, partner, None, None),
        (None, ahead, has_ahead, has_behind),
        (None, behind, has_behind, has_ahead),
        (0, behind, has_behind, has_ahead),
        (2, partner, has_ahead, has_far),
        (4, ahead, has_ahead & has_far, has_last),
    )

    def guarded(condition, action):
        if condition is None:
            action()
        else:
            pl.when(condition)(action)

    def send(slot, d):
        source, target, sends, _ = plan[slot]
        guarded(sends, lambda: copy(slot, source, d, target).start())

    def arrive(slot, d):
        source, target, _, receives = plan[slot]
        guarded(receives, lambda: copy(slot, source, d, target).wait_recv())

    def sent(slot, d):
        source, target, sends, _ = plan[slot]
        guarded(sends, lambda: copy(slot, source, d, target).wait_send())

    for d in range(owned):
        for slot in range(3):
            send(slot, d)

    def transform(slot, d):
        receives = plan[slot][3]

        def run():
            index = (SLOT_REL[slot] + REACH) * owned + d
            forward(window[slot, d], fwd_ref, twiddle_ref, spec_high, spec_low, index)

        guarded(receives, run)

    for d in range(owned):
        forward(slc_ref[d], fwd_ref, twiddle_ref, spec_high, spec_low, REACH * owned + d)

    line = lax.broadcasted_iota(jnp.int32, (RADIX * rows, 2 * SUB), 0)
    lane = lax.broadcasted_iota(jnp.int32, (RADIX * rows, 2 * SUB), 1)
    bins = (line // rows + RADIX * (lane % SUB) + RBLK // 2) % RBLK

    def filter_side(side):
        def step(p, carry):
            low_cut = cuts_ref[p, 0]
            high_cut = cuts_ref[p, 1]
            mask = jnp.where(
                (bins >= low_cut) & (bins < RBLK - high_cut), jnp.float32(1), jnp.float32(0)
            ).astype(jnp.bfloat16)
            date = pairs_ref[p, side]
            owner = date // owned
            index = (sign * (owner - me) + REACH) * owned + date - owner * owned
            index = jnp.clip(index, 0, spec_high.shape[0] - 1)
            tiles = inverse(spec_high[index], spec_low[index], mask, inv_ref, twiddle_ref, rows)
            for n, (re, im) in enumerate(tiles):
                fields_ref[side, p, 0, :, n * SUB : (n + 1) * SUB] = re.astype(jnp.bfloat16)
                fields_ref[side, p, 1, :, n * SUB : (n + 1) * SUB] = im.astype(jnp.bfloat16)
            return carry

        return step

    edge = pl.ds(pl.multiple_of((1 - pix) * (width - SUB), SUB), SUB)

    def edges(number, side, first, count):
        return pltpu.make_async_remote_copy(
            src_ref=fields_ref.at[side, pl.ds(first, count), :, :, edge],
            dst_ref=halo_ref.at[side, pl.ds(first, count)],
            send_sem=edge_send.at[number],
            recv_sem=edge_recv.at[number],
            device_id=(group, me, 1 - pix),
            device_id_type=MESH,
        )

    lax.fori_loop(0, pair_count, filter_side(0), 0)
    half = pair_count // 2
    edge_copies = [edges(0, 0, 0, pair_count), edges(1, 1, 0, half), edges(2, 1, half, half)]
    edge_copies[0].start()

    for d in range(owned):
        arrive(2, d)
        send(4, d)
        arrive(0, d)
        send(3, d)
    for slot in (2, 0):
        for d in range(owned):
            transform(slot, d)
    for d in range(owned):
        arrive(4, d)
        send(5, d)
    for d in range(owned):
        arrive(1, d)
        transform(1, d)
    for d in range(owned):
        transform(4, d)
    for slot in (3, 5):
        for d in range(owned):
            arrive(slot, d)
            transform(slot, d)

    lax.fori_loop(0, half, filter_side(1), 0)
    edge_copies[1].start()
    lax.fori_loop(half, pair_count, filter_side(1), 0)
    edge_copies[2].start()
    for slot in range(len(plan)):
        for d in range(owned):
            sent(slot, d)
    for item in edge_copies:
        item.wait()


def look_kernel(look_ref, fields_ref, halo_ref, interferogram_ref, coherence_ref):
    p = pl.program_id(0)
    rows, width = fields_ref.shape[-2:]
    pix = lax.axis_index("pix")
    half_az = look_ref[p, 0]
    half_range = look_ref[p, 1]

    def products(ref):
        ar, ai = (ref[0, 0, 0].astype(jnp.float32), ref[0, 0, 1].astype(jnp.float32))
        br, bi = (ref[1, 0, 0].astype(jnp.float32), ref[1, 0, 1].astype(jnp.float32))
        return split(
            jnp.concatenate(
                [ar * br + ai * bi, ai * br - ar * bi, ar * ar + ai * ai, br * br + bi * bi], 0
            )
        )

    on_left = jnp.where(pix == 1, jnp.float32(1), jnp.float32(0)).astype(jnp.bfloat16)
    on_right = jnp.where(pix == 0, jnp.float32(1), jnp.float32(0)).astype(jnp.bfloat16)
    extended = [
        jnp.concatenate([outer * on_left, inner, outer * on_right], 1)
        for inner, outer in zip(products(fields_ref), products(halo_ref))
    ]
    span = 2 * SUB
    first = lax.broadcasted_iota(jnp.int32, (span + 2 * SUB, span), 0)
    second = lax.broadcasted_iota(jnp.int32, (span + 2 * SUB, span), 1)
    one, zero = (jnp.float32(1), jnp.float32(0))
    range_band = jnp.where(jnp.abs(first - SUB - second) <= half_range, one, zero).astype(
        jnp.bfloat16
    )
    line = lax.broadcasted_iota(jnp.int32, (4 * rows, 4 * rows), 0)
    other = lax.broadcasted_iota(jnp.int32, (4 * rows, 4 * rows), 1)
    azimuth_band = jnp.where(
        (jnp.abs(line - other) <= half_az) & (line // rows == other // rows), one, zero
    ).astype(jnp.bfloat16)
    window_count = ((2 * half_az + 1) * (2 * half_range + 1)).astype(jnp.float32)
    scale = 1.0 / jnp.full((1, span), window_count, jnp.float32)
    for start in range(0, width, span):
        partial_sum = dot(extended[0][:, start : start + 2 * span], range_band) + dot(
            extended[1][:, start : start + 2 * span], range_band
        )
        high, low = split(partial_sum)
        sums = dot(azimuth_band, high) + dot(azimuth_band, low)
        re, im, first_power, second_power = [sums[q * rows : (q + 1) * rows] for q in range(4)]
        columns = slice(start, start + span)
        interferogram_ref[0, 0, :, columns] = re * scale
        interferogram_ref[0, 1, :, columns] = im * scale
        coherence_ref[0, :, columns] = jnp.sqrt(re * re + im * im) / (
            jnp.sqrt(first_power * second_power) + 0.25 * window_count
        )


def body(dates_dev, slc_tiles, pair_list, band_cuts, look_sizes):
    owned, _, rows, width = slc_tiles.shape
    pair_count = pair_list.shape[0]
    tables = [jnp.asarray(t) for t in dft_tables()]
    smem = pl.BlockSpec(memory_space=pltpu.SMEM)
    vmem = pl.BlockSpec(memory_space=pltpu.VMEM)
    slots = len(SLOT_REL)
    spectrum = (owned * (2 * REACH + 1), RADIX * rows, 2 * SUB)
    fields, halo = pl.pallas_call(
        functools.partial(field_kernel, dates_dev),
        out_shape=(
            jax.ShapeDtypeStruct((2, pair_count, 2, rows, width), jnp.bfloat16),
            jax.ShapeDtypeStruct((2, pair_count, 2, rows, SUB), jnp.bfloat16),
        ),
        in_specs=[smem, smem, vmem, vmem, vmem, vmem],
        out_specs=(vmem, vmem),
        scratch_shapes=[
            pltpu.VMEM((slots, owned, 2, rows, width), jnp.bfloat16),
            pltpu.VMEM(spectrum, jnp.bfloat16),
            pltpu.VMEM(spectrum, jnp.bfloat16),
            pltpu.SemaphoreType.DMA((slots, owned)),
            pltpu.SemaphoreType.DMA((slots, owned)),
            pltpu.SemaphoreType.DMA((3,)),
            pltpu.SemaphoreType.DMA((3,)),
        ],
        compiler_params=pltpu.CompilerParams(
            collective_id=0, has_side_effects=True, vmem_limit_bytes=40 * 1024 * 1024
        ),
        name="fields",
    )(pair_list, band_cuts, slc_tiles, *tables)
    return pl.pallas_call(
        look_kernel,
        grid=(pair_count,),
        out_shape=(
            jax.ShapeDtypeStruct((pair_count, 2, rows, width), jnp.float32),
            jax.ShapeDtypeStruct((pair_count, rows, width), jnp.float32),
        ),
        in_specs=[
            smem,
            pl.BlockSpec((2, 1, 2, rows, width), lambda p: (0, p, 0, 0, 0)),
            pl.BlockSpec((2, 1, 2, rows, SUB), lambda p: (0, p, 0, 0, 0)),
        ],
        out_specs=(
            pl.BlockSpec((1, 2, rows, width), lambda p: (p, 0, 0, 0)),
            pl.BlockSpec((1, rows, width), lambda p: (p, 0, 0)),
        ),
        compiler_params=pltpu.CompilerParams(vmem_limit_bytes=40 * 1024 * 1024),
        name="looks",
    )(look_sizes, fields, halo)


def solution(mesh):
    placed = (
        P(("groups", "date"), None, None, "pix"),
        P(("groups", "date"), None),
        P(("groups", "date"), None),
        P(("groups", "date"), None),
    )
    return jax.shard_map(
        functools.partial(body, mesh.shape["date"]),
        mesh=mesh,
        in_specs=placed,
        out_specs=(P(("groups", "date"), None, None, "pix"), P(("groups", "date"), None, "pix")),
        check_vma=False,
    )
```

time: 141 us -> 43.1 us (0.31)
  Pallas kernels: 0 us -> 36.2 us
  matrix products: 35.8 us -> 0 us
  other arithmetic: 26.9 us -> 0 us
  local copies, waits for them, and re-layouts: 28.5 us -> 5.79 us
  starting transfers between devices: 20.6 us -> 0 us
  waiting for transfers between devices: 16.7 us -> 0 us
  loops' own time: 10.7 us -> 0 us
    pallas_call x0 -> x2, Pallas kernels: none -> 36.2 us  [the longest x1 24.3 us: body(): pl.pallas_call(functools.partial(field_kernel, dates_dev), out_shape=(jax...]
    dot_general x19 -> x0, matrix products: 35.8 us -> none  [the longest x1 10.3 us: body(): jnp.dot(chosen * keep_both, inverse, precision=lax.Precision.HIGH)]
    ppermute x8 -> x0, starting transfers between devices: 20.6 us -> none  [the longest x6 15.4 us: shifted(): return lax.ppermute(x, axis, pairs)]
    ppermute x8 -> x0, waiting for transfers between devices: 16.7 us -> none  [the longest x6 15.4 us: shifted(): return lax.ppermute(x, axis, pairs)]
    dynamic_update_slice x16 -> x0, other arithmetic: 12 us -> none  [body(): interferogram, coherence = lax.map(multilook, (quantity, look_sizes))]
    another operation x1 -> x0, loops' own time: 10.7 us -> none  [body(): interferogram, coherence = lax.map(multilook, (quantity, look_sizes))]
    squeeze x8 -> x0, local copies, waits for them, and re-layouts: 9.04 us -> none  [body(): interferogram, coherence = lax.map(multilook, (quantity, look_sizes))]
    unnamed x20 -> x11, local copies, waits for them, and re-layouts: 0.15 us -> 5.79 us
  transfers between devices with their start and end apart: 8 -> 0, of which waited for: 2 -> 0; matrix products, arithmetic and copies ran while one was open for 7% -> 0% of each run, Pallas kernels for 0% -> 0%
where the time goes in v1:
time: 43.1 us; the launch traced here: 42.7 us
  Pallas kernels  36.2 us (84%)
  local copies, waits for them, and re-layouts  5.79 us (13%)
  between operations  0.64 us (1%)
    pallas_call x1, Pallas kernels, body(): pl.pallas_call(functools.partial(field_kernel, dates_dev), out_shape=(jax...  24.3 us
    pallas_call x1, Pallas kernels, body(): pl.pallas_call(look_kernel, grid=(pair_count,), out_shape=(jax.ShapeDtype...  11.9 us
    unnamed x11, local copies, waits for them, and re-layouts  5.79 us

profile of v1, /device:TPU:7, one launch (start us, length us, event | category | flops | bytes accessed | tf_op | source)
XLA Modules:
  0.0 42.7 jit_solution(1244910185757870874)
XLA Ops:
  0.6 0.8 %copy.9.pairs_ref = s32[8,2]{1,0:T(8,128)S(1)} copy(s32[8,2]{0,1:T(2,128)} %param.8) | data formatting | bytes 128 | tf_op args[1]
  1.4 0.8 %copy.10.cuts_ref = s32[8,2]{1,0:T(8,128)S(1)} copy(s32[8,2]{0,1:T(2,128)} %param.9) | data formatting | bytes 128 | tf_op args[2]
  2.1 0.8 %copy.11.look_ref = s32[8,2]{1,0:T(8,128)S(1)} copy(s32[8,2]{0,1:T(2,128)} %param.10) | data formatting | bytes 128 | tf_op args[3]
  2.9 0.0 copy-start
  2.9 0.9 %copy-done = bf16[2,2,64,512]{3,2,1,0:T(8,128)(2,1)S(1)} copy-done((bf16[2,2,64,512]{3,2,1,0:T(8,128)(2,1)S(1)}, bf16[2,2,64,512]{3,2,1,0:T(8,128)(2,1)}, u32[]{:S(2)}) %copy-start) | copy-done | bytes 262168
  3.8 0.0 copy-start.1
  3.8 0.9 %copy-done.1 = bf16[2,256,256]{2,1,0:T(8,128)(2,1)S(1)} copy-done((bf16[2,256,256]{2,1,0:T(8,128)(2,1)S(1)}, bf16[2,256,256]{2,1,0:T(8,128)(2,1)}, u32[]{:S(2)}) %copy-start.1) | copy-done | bytes 262168
  4.8 0.0 copy-start.2
  4.8 0.9 %copy-done.2 = bf16[2,256,256]{2,1,0:T(8,128)(2,1)S(1)} copy-done((bf16[2,256,256]{2,1,0:T(8,128)(2,1)S(1)}, bf16[2,256,256]{2,1,0:T(8,128)(2,1)}, u32[]{:S(2)}) %copy-start.2) | copy-done | bytes 262168
  5.7 0.0 copy-start.3
  5.7 0.7 %copy-done.3 = f32[2,4,128]{2,1,0:T(4,128)S(1)} copy-done((f32[2,4,128]{2,1,0:T(4,128)S(1)}, f32[2,4,128]{2,1,0:T(4,128)}, u32[]{:S(2)}) %copy-start.3) | copy-done | bytes 4120
  6.4 24.3 %fields.1 = (bf16[2,8,2,64,512]{4,3,2,1,0:T(8,128)(2,1)S(1)}, bf16[2,8,2,64,128]{4,3,2,1,0:T(8,128)(2,1)S(1)}) custom-call(s32[8,2]{1,0:T(8,128)S(1)} %copy.9.pairs_ref, s32[8,2]{1,0:T(8,128)S(1)} %copy.10.cuts_ref, bf16[2,2,64,512]{3,2,1,0:T(8,128)(2,1)S(1)} %copy-done, bf16[2,256,256]{2,1,0:T(8,128)(2,1)S(1)} %copy-done.2, ...), custom_call_target="tpu_custom_call" | custom-call | tf_op jit(solution)/shard_map/fields/pallas_call | solution.py:320
  30.7 11.9 %looks.1 = (f32[8,2,64,512]{3,2,1,0:T(8,128)}, f32[8,64,512]{2,1,0:T(8,128)}) custom-call(s32[8,2]{1,0:T(8,128)S(1)} %copy.11.look_ref, bf16[2,8,2,64,512]{4,3,2,1,0:T(8,128)(2,1)S(1)} %get-tuple-element.4.fields_ref, bf16[2,8,2,64,128]{4,3,2,1,0:T(8,128)(2,1)S(1)} %get-tuple-element.5.halo_ref), custom_call_target="tpu_custom_call" | custom-call | tf_op jit(solution)/shard_map/looks/pallas_call | solution.py:342
Async XLA Ops:
  2.9 0.9 %copy-start = (bf16[2,2,64,512]{3,2,1,0:T(8,128)(2,1)S(1)}, bf16[2,2,64,512]{3,2,1,0:T(8,128)(2,1)}, u32[]{:S(2)}) copy-start(bf16[2,2,64,512]{3,2,1,0:T(8,128)(2,1)} %slc_ref.1) | copy-start | bytes 786436
  3.8 0.9 %copy-start.1 = (bf16[2,256,256]{2,1,0:T(8,128)(2,1)S(1)}, bf16[2,256,256]{2,1,0:T(8,128)(2,1)}, u32[]{:S(2)}) copy-start(bf16[2,256,256]{2,1,0:T(8,128)(2,1)} %constant.7.clone.inv_ref) | copy-start | bytes 786436
  4.8 0.9 %copy-start.2 = (bf16[2,256,256]{2,1,0:T(8,128)(2,1)S(1)}, bf16[2,256,256]{2,1,0:T(8,128)(2,1)}, u32[]{:S(2)}) copy-start(bf16[2,256,256]{2,1,0:T(8,128)(2,1)} %constant.6.clone.fwd_ref) | copy-start | bytes 786436
  5.7 0.7 %copy-start.3 = (f32[2,4,128]{2,1,0:T(4,128)S(1)}, f32[2,4,128]{2,1,0:T(4,128)}, u32[]{:S(2)}) copy-start(f32[2,4,128]{2,1,0:T(4,128)} %constant.8.clone.twiddle_ref) | copy-start | bytes 12292

commit v2 on v1

--- a/solution.py
+++ b/solution.py
@@ -13,6 +13,8 @@
 SUB = 128
 RADIX = RBLK // SUB
 REACH = 3
+UNROLL = 4
+GROUP = 2
 SLOT_REL = (1, -2, 2, 3, -1, -3)
 
 
@@ -48,25 +50,27 @@
     return dot(high, table[0]) + dot(low, table[0]) + dot(high, table[1])
 
 
-def forward(image, table, twiddle, high_ref, low_ref, index):
-    rows = image.shape[1]
-    re = [image[0, :, n * SUB : (n + 1) * SUB].astype(jnp.float32) for n in range(RADIX)]
-    im = [image[1, :, n * SUB : (n + 1) * SUB].astype(jnp.float32) for n in range(RADIX)]
-    sr, si = (re[0] + re[2], im[0] + im[2])
-    dr, di = (re[0] - re[2], im[0] - im[2])
-    tr, ti = (re[1] + re[3], im[1] + im[3])
-    er, ei = (re[1] - re[3], im[1] - im[3])
-    parts = [(sr + tr, si + ti), (dr + ei, di - er), (sr - tr, si - ti), (dr - ei, di + er)]
+def forward(images, table, twiddle, high_ref, low_ref, start):
     turned = []
-    for k, (pr, pi) in enumerate(parts):
-        c, s = (twiddle[0, k : k + 1, :], twiddle[1, k : k + 1, :])
-        turned.append(
-            jnp.concatenate([pr, pi] if k == 0 else [pr * c - pi * s, pr * s + pi * c], 1)
-        )
+    for image in images:
+        re = [image[0, :, n * SUB : (n + 1) * SUB].astype(jnp.float32) for n in range(RADIX)]
+        im = [image[1, :, n * SUB : (n + 1) * SUB].astype(jnp.float32) for n in range(RADIX)]
+        sr, si = (re[0] + re[2], im[0] + im[2])
+        dr, di = (re[0] - re[2], im[0] - im[2])
+        tr, ti = (re[1] + re[3], im[1] + im[3])
+        er, ei = (re[1] - re[3], im[1] - im[3])
+        parts = [(sr + tr, si + ti), (dr + ei, di - er), (sr - tr, si - ti), (dr - ei, di + er)]
+        for k, (pr, pi) in enumerate(parts):
+            c, s = (twiddle[0, k : k + 1, :], twiddle[1, k : k + 1, :])
+            turned.append(
+                jnp.concatenate([pr, pi] if k == 0 else [pr * c - pi * s, pr * s + pi * c], 1)
+            )
     high, low = split(jnp.concatenate(turned, 0))
     high, low = split(dot3(high, low, table))
-    high_ref[index] = high
-    low_ref[index] = low
+    count = high.shape[0] // len(images)
+    for d in range(len(images)):
+        high_ref[start + d] = high[d * count : (d + 1) * count]
+        low_ref[start + d] = low[d * count : (d + 1) * count]
 
 
 def inverse(high, low, mask, table, twiddle, rows):
@@ -90,11 +94,13 @@
     pairs_ref,
     cuts_ref,
     slc_ref,
-    fwd_ref,
-    inv_ref,
-    twiddle_ref,
+    tables_hbm,
+    twiddle_hbm,
     fields_ref,
     halo_ref,
+    own_ref,
+    tables_ref,
+    twiddle_ref,
     window,
     spec_high,
     spec_low,
@@ -102,9 +108,19 @@
     recv_sem,
     edge_send,
     edge_recv,
+    load_sem,
 ):
     owned, _, rows, width = slc_ref.shape
-    pair_count = pairs_ref.shape[0]
+    pair_count = pairs_ref.shape[1]
+    loads = [
+        pltpu.make_async_copy(src, dst, load_sem.at[n])
+        for n, (src, dst) in enumerate(
+            ((slc_ref, own_ref), (tables_hbm, tables_ref), (twiddle_hbm, twiddle_ref))
+        )
+    ]
+    for item in loads:
+        item.start()
+    fwd_ref, inv_ref = (tables_ref.at[0], tables_ref.at[1])
     group = lax.axis_index("groups")
     me = lax.axis_index("date")
     pix = lax.axis_index("pix")
@@ -174,17 +190,18 @@
         for slot in range(3):
             send(slot, d)
 
-    def transform(slot, d):
-        receives = plan[slot][3]
-
+    def transform(slot):
         def run():
-            index = (SLOT_REL[slot] + REACH) * owned + d
-            forward(window[slot, d], fwd_ref, twiddle_ref, spec_high, spec_low, index)
-
-        guarded(receives, run)
-
-    for d in range(owned):
-        forward(slc_ref[d], fwd_ref, twiddle_ref, spec_high, spec_low, REACH * owned + d)
+            images = [window[slot, d] for d in range(owned)]
+            start = (SLOT_REL[slot] + REACH) * owned
+            forward(images, fwd_ref, twiddle_ref, spec_high, spec_low, start)
+
+        guarded(plan[slot][3], run)
+
+    for item in loads:
+        item.wait()
+    own = [own_ref[d] for d in range(owned)]
+    forward(own, fwd_ref, twiddle_ref, spec_high, spec_low, REACH * owned)
 
     line = lax.broadcasted_iota(jnp.int32, (RADIX * rows, 2 * SUB), 0)
     lane = lax.broadcasted_iota(jnp.int32, (RADIX * rows, 2 * SUB), 1)
@@ -192,12 +209,12 @@
 
     def filter_side(side):
         def step(p, carry):
-            low_cut = cuts_ref[p, 0]
-            high_cut = cuts_ref[p, 1]
+            low_cut = cuts_ref[0, p]
+            high_cut = cuts_ref[1, p]
             mask = jnp.where(
                 (bins >= low_cut) & (bins < RBLK - high_cut), jnp.float32(1), jnp.float32(0)
             ).astype(jnp.bfloat16)
-            date = pairs_ref[p, side]
+            date = pairs_ref[side, p]
             owner = date // owned
             index = (sign * (owner - me) + REACH) * owned + date - owner * owned
             index = jnp.clip(index, 0, spec_high.shape[0] - 1)
@@ -221,7 +238,7 @@
             device_id_type=MESH,
         )
 
-    lax.fori_loop(0, pair_count, filter_side(0), 0)
+    lax.fori_loop(0, pair_count, filter_side(0), 0, unroll=UNROLL)
     half = pair_count // 2
     edge_copies = [edges(0, 0, 0, pair_count), edges(1, 1, 0, half), edges(2, 1, half, half)]
     edge_copies[0].start()
@@ -231,25 +248,23 @@
         send(4, d)
         arrive(0, d)
         send(3, d)
-    for slot in (2, 0):
-        for d in range(owned):
-            transform(slot, d)
+    transform(2)
+    transform(0)
     for d in range(owned):
         arrive(4, d)
         send(5, d)
     for d in range(owned):
         arrive(1, d)
-        transform(1, d)
-    for d in range(owned):
-        transform(4, d)
+    transform(1)
+    transform(4)
     for slot in (3, 5):
         for d in range(owned):
             arrive(slot, d)
-            transform(slot, d)
-
-    lax.fori_loop(0, half, filter_side(1), 0)
+        transform(slot)
+
+    lax.fori_loop(0, half, filter_side(1), 0, unroll=UNROLL)
     edge_copies[1].start()
-    lax.fori_loop(half, pair_count, filter_side(1), 0)
+    lax.fori_loop(half, pair_count, filter_side(1), 0, unroll=UNROLL)
     edge_copies[2].start()
     for slot in range(len(plan)):
         for d in range(owned):
@@ -259,60 +274,59 @@
 
 
 def look_kernel(look_ref, fields_ref, halo_ref, interferogram_ref, coherence_ref):
-    p = pl.program_id(0)
+    step = pl.program_id(0)
     rows, width = fields_ref.shape[-2:]
     pix = lax.axis_index("pix")
-    half_az = look_ref[p, 0]
-    half_range = look_ref[p, 1]
-
-    def products(ref):
-        ar, ai = (ref[0, 0, 0].astype(jnp.float32), ref[0, 0, 1].astype(jnp.float32))
-        br, bi = (ref[1, 0, 0].astype(jnp.float32), ref[1, 0, 1].astype(jnp.float32))
-        return split(
-            jnp.concatenate(
-                [ar * br + ai * bi, ai * br - ar * bi, ar * ar + ai * ai, br * br + bi * bi], 0
-            )
-        )
-
-    on_left = jnp.where(pix == 1, jnp.float32(1), jnp.float32(0)).astype(jnp.bfloat16)
-    on_right = jnp.where(pix == 0, jnp.float32(1), jnp.float32(0)).astype(jnp.bfloat16)
-    extended = [
-        jnp.concatenate([outer * on_left, inner, outer * on_right], 1)
-        for inner, outer in zip(products(fields_ref), products(halo_ref))
-    ]
+
+    def products(ref, g):
+        ar, ai = (ref[0, g, 0].astype(jnp.float32), ref[0, g, 1].astype(jnp.float32))
+        br, bi = (ref[1, g, 0].astype(jnp.float32), ref[1, g, 1].astype(jnp.float32))
+        return jnp.concatenate(
+            [ar * br + ai * bi, ai * br - ar * bi, ar * ar + ai * ai, br * br + bi * bi], 0
+        ).astype(jnp.bfloat16)
+
+    def root(x):
+        return x * lax.rsqrt(jnp.maximum(x, jnp.float32(1e-37)))
+
+    one, zero = (jnp.float32(1), jnp.float32(0))
+    on_left = jnp.where(pix == 1, one, zero).astype(jnp.bfloat16)
+    on_right = jnp.where(pix == 0, one, zero).astype(jnp.bfloat16)
     span = 2 * SUB
     first = lax.broadcasted_iota(jnp.int32, (span + 2 * SUB, span), 0)
     second = lax.broadcasted_iota(jnp.int32, (span + 2 * SUB, span), 1)
-    one, zero = (jnp.float32(1), jnp.float32(0))
-    range_band = jnp.where(jnp.abs(first - SUB - second) <= half_range, one, zero).astype(
-        jnp.bfloat16
-    )
+    range_gap = jnp.abs(first - SUB - second)
     line = lax.broadcasted_iota(jnp.int32, (4 * rows, 4 * rows), 0)
     other = lax.broadcasted_iota(jnp.int32, (4 * rows, 4 * rows), 1)
-    azimuth_band = jnp.where(
-        (jnp.abs(line - other) <= half_az) & (line // rows == other // rows), one, zero
-    ).astype(jnp.bfloat16)
-    window_count = ((2 * half_az + 1) * (2 * half_range + 1)).astype(jnp.float32)
-    scale = 1.0 / jnp.full((1, span), window_count, jnp.float32)
-    for start in range(0, width, span):
-        partial_sum = dot(extended[0][:, start : start + 2 * span], range_band) + dot(
-            extended[1][:, start : start + 2 * span], range_band
-        )
-        high, low = split(partial_sum)
-        sums = dot(azimuth_band, high) + dot(azimuth_band, low)
-        re, im, first_power, second_power = [sums[q * rows : (q + 1) * rows] for q in range(4)]
-        columns = slice(start, start + span)
-        interferogram_ref[0, 0, :, columns] = re * scale
-        interferogram_ref[0, 1, :, columns] = im * scale
-        coherence_ref[0, :, columns] = jnp.sqrt(re * re + im * im) / (
-            jnp.sqrt(first_power * second_power) + 0.25 * window_count
-        )
+    azimuth_gap = jnp.where(line // rows == other // rows, jnp.abs(line - other), rows)
+    for g in range(fields_ref.shape[1]):
+        half_az = look_ref[0, step * fields_ref.shape[1] + g]
+        half_range = look_ref[1, step * fields_ref.shape[1] + g]
+        outer = products(halo_ref, g)
+        extended = jnp.concatenate(
+            [outer * on_left, products(fields_ref, g), outer * on_right], 1
+        )
+        range_band = jnp.where(range_gap <= half_range, one, zero).astype(jnp.bfloat16)
+        azimuth_band = jnp.where(azimuth_gap <= half_az, one, zero).astype(jnp.bfloat16)
+        window_count = ((2 * half_az + 1) * (2 * half_range + 1)).astype(jnp.float32)
+        scale = 1.0 / jnp.full((1, span), window_count, jnp.float32)
+        for start in range(0, width, span):
+            partial_sum = dot(extended[:, start : start + 2 * span], range_band)
+            sums = dot(azimuth_band, partial_sum.astype(jnp.bfloat16))
+            re, im, first_power, second_power = [sums[q * rows : (q + 1) * rows] for q in range(4)]
+            columns = slice(start, start + span)
+            interferogram_ref[g, 0, :, columns] = re * scale
+            interferogram_ref[g, 1, :, columns] = im * scale
+            coherence_ref[g, :, columns] = root(re * re + im * im) / (
+                root(first_power * second_power) + 0.25 * window_count
+            )
 
 
 def body(dates_dev, slc_tiles, pair_list, band_cuts, look_sizes):
     owned, _, rows, width = slc_tiles.shape
     pair_count = pair_list.shape[0]
-    tables = [jnp.asarray(t) for t in dft_tables()]
+    forward_table, inverse_table, twiddle = dft_tables()
+    tables = jnp.asarray(np.stack([forward_table, inverse_table]))
+    hbm = pl.BlockSpec(memory_space=pltpu.HBM)
     smem = pl.BlockSpec(memory_space=pltpu.SMEM)
     vmem = pl.BlockSpec(memory_space=pltpu.VMEM)
     slots = len(SLOT_REL)
@@ -323,9 +337,12 @@
             jax.ShapeDtypeStruct((2, pair_count, 2, rows, width), jnp.bfloat16),
             jax.ShapeDtypeStruct((2, pair_count, 2, rows, SUB), jnp.bfloat16),
         ),
-        in_specs=[smem, smem, vmem, vmem, vmem, vmem],
+        in_specs=[smem, smem, hbm, hbm, hbm],
         out_specs=(vmem, vmem),
         scratch_shapes=[
+            pltpu.VMEM(slc_tiles.shape, slc_tiles.dtype),
+            pltpu.VMEM(tables.shape, tables.dtype),
+            pltpu.VMEM(twiddle.shape, twiddle.dtype),
             pltpu.VMEM((slots, owned, 2, rows, width), jnp.bfloat16),
             pltpu.VMEM(spectrum, jnp.bfloat16),
             pltpu.VMEM(spectrum, jnp.bfloat16),
@@ -333,31 +350,32 @@
             pltpu.SemaphoreType.DMA((slots, owned)),
             pltpu.SemaphoreType.DMA((3,)),
             pltpu.SemaphoreType.DMA((3,)),
+            pltpu.SemaphoreType.DMA((3,)),
         ],
         compiler_params=pltpu.CompilerParams(
             collective_id=0, has_side_effects=True, vmem_limit_bytes=40 * 1024 * 1024
         ),
         name="fields",
-    )(pair_list, band_cuts, slc_tiles, *tables)
+    )(pair_list.T, band_cuts.T, slc_tiles, tables, jnp.asarray(twiddle))
     return pl.pallas_call(
         look_kernel,
-        grid=(pair_count,),
+        grid=(pair_count // GROUP,),
         out_shape=(
             jax.ShapeDtypeStruct((pair_count, 2, rows, width), jnp.float32),
             jax.ShapeDtypeStruct((pair_count, rows, width), jnp.float32),
         ),
         in_specs=[
             smem,
-            pl.BlockSpec((2, 1, 2, rows, width), lambda p: (0, p, 0, 0, 0)),
-            pl.BlockSpec((2, 1, 2, rows, SUB), lambda p: (0, p, 0, 0, 0)),
+            pl.BlockSpec((2, GROUP, 2, rows, width), lambda p: (0, p, 0, 0, 0)),
+            pl.BlockSpec((2, GROUP, 2, rows, SUB), lambda p: (0, p, 0, 0, 0)),
         ],
         out_specs=(
-            pl.BlockSpec((1, 2, rows, width), lambda p: (p, 0, 0, 0)),
-            pl.BlockSpec((1, rows, width), lambda p: (p, 0, 0)),
+            pl.BlockSpec((GROUP, 2, rows, width), lambda p: (p, 0, 0, 0)),
+            pl.BlockSpec((GROUP, rows, width), lambda p: (p, 0, 0)),
         ),
         compiler_params=pltpu.CompilerParams(vmem_limit_bytes=40 * 1024 * 1024),
         name="looks",
-    )(look_sizes, fields, halo)
+    )(look_sizes.T, fields, halo)
 
 
 def solution(mesh):

time: 43.1 us -> 36.7 us (0.85)
  Pallas kernels: 36.2 us -> 30.9 us
  local copies, waits for them, and re-layouts: 5.79 us -> 4.7 us
    pallas_call x1, Pallas kernels: 11.9 us -> 7.56 us  [body(): pl.pallas_call(look_kernel, grid=(pair_count // GROUP,), out_shape=(jax.S...]
    unnamed x11 -> x12, local copies, waits for them, and re-layouts: 5.79 us -> 4.7 us
    pallas_call x1, Pallas kernels: 24.3 us -> 23.3 us  [body(): pl.pallas_call(functools.partial(field_kernel, dates_dev), out_shape=(jax...]
where the time goes in v2:
time: 36.7 us; the launch traced here: 36.2 us
  Pallas kernels  30.9 us (84%)
  local copies, waits for them, and re-layouts  4.7 us (13%)
  between operations  0.66 us (2%)
    pallas_call x1, Pallas kernels, body(): pl.pallas_call(functools.partial(field_kernel, dates_dev), out_shape=(jax...  23.3 us
    pallas_call x1, Pallas kernels, body(): pl.pallas_call(look_kernel, grid=(pair_count // GROUP,), out_shape=(jax.S...  7.56 us
    unnamed x12, local copies, waits for them, and re-layouts  4.7 us

profile of v2, /device:TPU:7, one launch (start us, length us, event | category | flops | bytes accessed | tf_op | source)
XLA Modules:
  0.0 36.2 jit_solution(9588756050950060235)
XLA Ops:
  0.6 0.0 copy-start
  0.6 1.0 %copy-done = bf16[2,2,256,256]{3,2,1,0:T(8,128)(2,1)S(1)} copy-done((bf16[2,2,256,256]{3,2,1,0:T(8,128)(2,1)S(1)}, bf16[2,2,256,256]{3,2,1,0:T(8,128)(2,1)}, u32[]{:S(2)}) %copy-start) | copy-done | bytes 524312
  1.7 0.0 copy-start.1
  1.7 0.9 %copy-done.1 = bf16[2,2,64,512]{3,2,1,0:T(8,128)(2,1)S(1)} copy-done((bf16[2,2,64,512]{3,2,1,0:T(8,128)(2,1)S(1)}, bf16[2,2,64,512]{3,2,1,0:T(8,128)(2,1)}, u32[]{:S(2)}) %copy-start.1) | copy-done | bytes 262168
  2.6 0.0 copy-start.2
  2.6 0.7 %copy-done.2 = f32[2,4,128]{2,1,0:T(4,128)S(1)} copy-done((f32[2,4,128]{2,1,0:T(4,128)S(1)}, f32[2,4,128]{2,1,0:T(4,128)}, u32[]{:S(2)}) %copy-start.2) | copy-done | bytes 4120
  3.3 0.0 copy-start.3
  3.3 0.7 %copy-done.3 = s32[8,2]{0,1:T(2,128)S(1)} copy-done((s32[8,2]{0,1:T(2,128)S(1)}, s32[8,2]{0,1:T(2,128)}, u32[]{:S(2)}) %copy-start.3) | copy-done | bytes 88
  4.0 0.0 copy-start.4
  4.0 0.7 %copy-done.4 = s32[8,2]{0,1:T(2,128)S(1)} copy-done((s32[8,2]{0,1:T(2,128)S(1)}, s32[8,2]{0,1:T(2,128)}, u32[]{:S(2)}) %copy-start.4) | copy-done | bytes 88
  4.7 23.3 %fields.1 = (bf16[2,8,2,64,512]{4,3,2,1,0:T(8,128)(2,1)S(1)}, bf16[2,8,2,64,128]{4,3,2,1,0:T(8,128)(2,1)S(1)}) custom-call(s32[2,8]{1,0:T(2,128)S(1)} %bitcast.3, s32[2,8]{1,0:T(2,128)S(1)} %bitcast.4, bf16[2,2,64,512]{3,2,1,0:T(8,128)(2,1)S(1)} %copy-done.1, bf16[2,2,256,256]{3,2,1,0:T(8,128)(2,1)S(1)} %copy-done, f32[2,4,128]{2,1,0:T(4,128)S(1)} %copy-done.2), custom_call_target="tpu_custom_call" | custom-call | tf_op jit(solution)/shard_map/fields/pallas_call | solution.py:334
  28.0 0.0 copy-start.5
  28.0 0.7 %copy-done.5 = s32[8,2]{0,1:T(2,128)S(1)} copy-done((s32[8,2]{0,1:T(2,128)S(1)}, s32[8,2]{0,1:T(2,128)}, u32[]{:S(2)}) %copy-start.5) | copy-done | bytes 88
  28.7 7.6 %looks.1 = (f32[8,2,64,512]{3,2,1,0:T(8,128)}, f32[8,64,512]{2,1,0:T(8,128)}) custom-call(s32[2,8]{1,0:T(2,128)S(1)} %bitcast.5, bf16[2,8,2,64,512]{4,3,2,1,0:T(8,128)(2,1)S(1)} %get-tuple-element.4.fields_ref, bf16[2,8,2,64,128]{4,3,2,1,0:T(8,128)(2,1)S(1)} %get-tuple-element.5.halo_ref), custom_call_target="tpu_custom_call" | custom-call | tf_op jit(solution)/shard_map/looks/pallas_call | solution.py:360
Async XLA Ops:
  0.6 1.0 %copy-start = (bf16[2,2,256,256]{3,2,1,0:T(8,128)(2,1)S(1)}, bf16[2,2,256,256]{3,2,1,0:T(8,128)(2,1)}, u32[]{:S(2)}) copy-start(bf16[2,2,256,256]{3,2,1,0:T(8,128)(2,1)} %constant.4.clone.tables_hbm) | copy-start | bytes 1572868
  1.7 0.9 %copy-start.1 = (bf16[2,2,64,512]{3,2,1,0:T(8,128)(2,1)S(1)}, bf16[2,2,64,512]{3,2,1,0:T(8,128)(2,1)}, u32[]{:S(2)}) copy-start(bf16[2,2,64,512]{3,2,1,0:T(8,128)(2,1)} %slc_ref.1) | copy-start | bytes 786436
  2.6 0.7 %copy-start.2 = (f32[2,4,128]{2,1,0:T(4,128)S(1)}, f32[2,4,128]{2,1,0:T(4,128)}, u32[]{:S(2)}) copy-start(f32[2,4,128]{2,1,0:T(4,128)} %constant.5.clone.twiddle_hbm) | copy-start | bytes 12292
  3.3 0.7 %copy-start.3 = (s32[8,2]{0,1:T(2,128)S(1)}, s32[8,2]{0,1:T(2,128)}, u32[]{:S(2)}) copy-start(s32[8,2]{0,1:T(2,128)} %param.7) | copy-start | bytes 196
  4.0 0.7 %copy-start.4 = (s32[8,2]{0,1:T(2,128)S(1)}, s32[8,2]{0,1:T(2,128)}, u32[]{:S(2)}) copy-start(s32[8,2]{0,1:T(2,128)} %param.8) | copy-start | bytes 196
  28.0 0.7 %copy-start.5 = (s32[8,2]{0,1:T(2,128)S(1)}, s32[8,2]{0,1:T(2,128)}, u32[]{:S(2)}) copy-start(s32[8,2]{0,1:T(2,128)} %param.9) | copy-start | bytes 196

commit v3 on v2

--- a/solution.py
+++ b/solution.py
@@ -148,13 +148,14 @@
     pl.when(has_behind)(lambda: greet(behind, pix))
     pl.semaphore_wait(barrier, 2 + has_ahead.astype(jnp.int32) + has_behind.astype(jnp.int32))
 
-    def copy(slot, source, d, target):
-        src = slc_ref.at[d] if source is None else window.at[source, d]
+    def copy(slot, source, c, target):
+        d, half = divmod(c, 2)
+        src = slc_ref.at[d, half] if source is None else window.at[source, d, half]
         return pltpu.make_async_remote_copy(
             src_ref=src,
-            dst_ref=window.at[slot, d],
-            send_sem=send_sem.at[slot, d],
-            recv_sem=recv_sem.at[slot, d],
+            dst_ref=window.at[slot, d, half],
+            send_sem=send_sem.at[slot, c],
+            recv_sem=recv_sem.at[slot, c],
             device_id=(group, target, pix),
             device_id_type=MESH,
         )
@@ -186,9 +187,10 @@
         source, target, sends, _ = plan[slot]
         guarded(sends, lambda: copy(slot, source, d, target).wait_send())
 
-    for d in range(owned):
-        for slot in range(3):
-            send(slot, d)
+    chunks = 2 * owned
+    for c in range(chunks):
+        for slot in (2, 1, 0):
+            send(slot, c)
 
     def transform(slot):
         def run():
@@ -238,28 +240,33 @@
             device_id_type=MESH,
         )
 
-    lax.fori_loop(0, pair_count, filter_side(0), 0, unroll=UNROLL)
     half = pair_count // 2
     edge_copies = [edges(0, 0, 0, pair_count), edges(1, 1, 0, half), edges(2, 1, half, half)]
+    def relay(c):
+        arrive(4, c)
+        send(5, c)
+
+    share = pair_count // chunks
+    for c in range(chunks):
+        lax.fori_loop(c * share, (c + 1) * share, filter_side(0), 0, unroll=2)
+        arrive(2, c)
+        send(4, c)
+        arrive(0, c)
+        send(3, c)
+        if c >= 2:
+            relay(c - 2)
     edge_copies[0].start()
-
-    for d in range(owned):
-        arrive(2, d)
-        send(4, d)
-        arrive(0, d)
-        send(3, d)
+    relay(chunks - 2)
     transform(2)
+    relay(chunks - 1)
     transform(0)
-    for d in range(owned):
-        arrive(4, d)
-        send(5, d)
-    for d in range(owned):
-        arrive(1, d)
+    for c in range(chunks):
+        arrive(1, c)
     transform(1)
     transform(4)
     for slot in (3, 5):
-        for d in range(owned):
-            arrive(slot, d)
+        for c in range(chunks):
+            arrive(slot, c)
         transform(slot)
 
     lax.fori_loop(0, half, filter_side(1), 0, unroll=UNROLL)
@@ -267,8 +274,8 @@
     lax.fori_loop(half, pair_count, filter_side(1), 0, unroll=UNROLL)
     edge_copies[2].start()
     for slot in range(len(plan)):
-        for d in range(owned):
-            sent(slot, d)
+        for c in range(chunks):
+            sent(slot, c)
     for item in edge_copies:
         item.wait()
 
@@ -346,14 +353,14 @@
             pltpu.VMEM((slots, owned, 2, rows, width), jnp.bfloat16),
             pltpu.VMEM(spectrum, jnp.bfloat16),
             pltpu.VMEM(spectrum, jnp.bfloat16),
-            pltpu.SemaphoreType.DMA((slots, owned)),
-            pltpu.SemaphoreType.DMA((slots, owned)),
+            pltpu.SemaphoreType.DMA((slots, 2 * owned)),
+            pltpu.SemaphoreType.DMA((slots, 2 * owned)),
             pltpu.SemaphoreType.DMA((3,)),
             pltpu.SemaphoreType.DMA((3,)),
             pltpu.SemaphoreType.DMA((3,)),
         ],
         compiler_params=pltpu.CompilerParams(
-            collective_id=0, has_side_effects=True, vmem_limit_bytes=40 * 1024 * 1024
+            collective_id=0, has_side_effects=True, vmem_limit_bytes=56 * 1024 * 1024
         ),
         name="fields",
     )(pair_list.T, band_cuts.T, slc_tiles, tables, jnp.asarray(twiddle))
@@ -373,7 +380,7 @@
             pl.BlockSpec((GROUP, 2, rows, width), lambda p: (p, 0, 0, 0)),
             pl.BlockSpec((GROUP, rows, width), lambda p: (p, 0, 0)),
         ),
-        compiler_params=pltpu.CompilerParams(vmem_limit_bytes=40 * 1024 * 1024),
+        compiler_params=pltpu.CompilerParams(vmem_limit_bytes=56 * 1024 * 1024),
         name="looks",
     )(look_sizes.T, fields, halo)
 

time: 36.7 us -> 33.9 us (0.924)
  local copies, waits for them, and re-layouts: 4.7 us -> 0 us
  Pallas kernels: 30.9 us -> 33.1 us
    unnamed x12 -> x0, local copies, waits for them, and re-layouts: 4.7 us -> none
    pallas_call x1, Pallas kernels: 23.3 us -> 25.1 us  [body(): pl.pallas_call(functools.partial(field_kernel, dates_dev), out_shape=(jax...]
    pallas_call x1, Pallas kernels: 7.56 us -> 7.98 us  [body(): pl.pallas_call(look_kernel, grid=(pair_count // GROUP,), out_shape=(jax.S...]
where the time goes in v3:
time: 33.9 us; the launch traced here: 33.7 us
  Pallas kernels  33.1 us (98%)
  between operations  0.64 us (2%)
    pallas_call x1, Pallas kernels, body(): pl.pallas_call(functools.partial(field_kernel, dates_dev), out_shape=(jax...  25.1 us
    pallas_call x1, Pallas kernels, body(): pl.pallas_call(look_kernel, grid=(pair_count // GROUP,), out_shape=(jax.S...  7.98 us

profile of v3, /device:TPU:7, one launch (start us, length us, event | category | flops | bytes accessed | tf_op | source)
XLA Modules:
  0.0 33.7 jit_solution(4840173235452602455)
XLA Ops:
  0.6 25.1 %fields.1 = (bf16[2,8,2,64,512]{4,3,2,1,0:T(8,128)(2,1)}, bf16[2,8,2,64,128]{4,3,2,1,0:T(8,128)(2,1)}) custom-call(s32[2,8]{1,0:T(2,128)} %bitcast.3, s32[2,8]{1,0:T(2,128)} %bitcast.4, bf16[2,2,64,512]{3,2,1,0:T(8,128)(2,1)} %slc_ref.1, bf16[2,2,256,256]{3,2,1,0:T(8,128)(2,1)} %constant.4.clone.tables_hbm, f32[2,4,128]{2,1,0:T(4,128)} %constant.5.clone.twiddle_hbm), custom_call_target="tpu_custom_call" | custom-call | tf_op jit(solution)/shard_map/fields/pallas_call | solution.py:341
  25.8 8.0 %looks.1 = (f32[8,2,64,512]{3,2,1,0:T(8,128)}, f32[8,64,512]{2,1,0:T(8,128)}) custom-call(s32[2,8]{1,0:T(2,128)} %bitcast.5, bf16[2,8,2,64,512]{4,3,2,1,0:T(8,128)(2,1)} %get-tuple-element.4.fields_ref, bf16[2,8,2,64,128]{4,3,2,1,0:T(8,128)(2,1)} %get-tuple-element.5.halo_ref), custom_call_target="tpu_custom_call" | custom-call | tf_op jit(solution)/shard_map/looks/pallas_call | solution.py:367

commit v4 on v3

--- a/solution.py
+++ b/solution.py
@@ -14,7 +14,7 @@
 RADIX = RBLK // SUB
 REACH = 3
 UNROLL = 4
-GROUP = 2
+GROUP = 4
 SLOT_REL = (1, -2, 2, 3, -1, -3)
 
 

time: 33.9 us -> 33.9 us (level)
  no operation moved by 1% of the time
where the time goes in v4:
time: 33.9 us; the launch traced here: 33.7 us
  Pallas kernels  33.1 us (98%)
  between operations  0.64 us (2%)
    pallas_call x1, Pallas kernels, body(): pl.pallas_call(functools.partial(field_kernel, dates_dev), out_shape=(jax...  25.1 us
    pallas_call x1, Pallas kernels, body(): pl.pallas_call(look_kernel, grid=(pair_count // GROUP,), out_shape=(jax.S...  7.98 us

profile of v4, /device:TPU:7, one launch (start us, length us, event | category | flops | bytes accessed | tf_op | source)
XLA Modules:
  0.0 33.7 jit_solution(18376666840233842948)
XLA Ops:
  0.6 25.1 %fields.1 = (bf16[2,8,2,64,512]{4,3,2,1,0:T(8,128)(2,1)}, bf16[2,8,2,64,128]{4,3,2,1,0:T(8,128)(2,1)}) custom-call(s32[2,8]{1,0:T(2,128)} %bitcast.3, s32[2,8]{1,0:T(2,128)} %bitcast.4, bf16[2,2,64,512]{3,2,1,0:T(8,128)(2,1)} %slc_ref.1, bf16[2,2,256,256]{3,2,1,0:T(8,128)(2,1)} %constant.4.clone.tables_hbm, f32[2,4,128]{2,1,0:T(4,128)} %constant.5.clone.twiddle_hbm), custom_call_target="tpu_custom_call" | custom-call | tf_op jit(solution)/shard_map/fields/pallas_call | solution.py:341
  25.8 8.0 %looks.1 = (f32[8,2,64,512]{3,2,1,0:T(8,128)}, f32[8,64,512]{2,1,0:T(8,128)}) custom-call(s32[2,8]{1,0:T(2,128)} %bitcast.5, bf16[2,8,2,64,512]{4,3,2,1,0:T(8,128)(2,1)} %get-tuple-element.4.fields_ref, bf16[2,8,2,64,128]{4,3,2,1,0:T(8,128)(2,1)} %get-tuple-element.5.halo_ref), custom_call_target="tpu_custom_call" | custom-call | tf_op jit(solution)/shard_map/looks/pallas_call | solution.py:367
